TPU v7x, 32 devices: a whole 2x2x4 slice. The times are simulated.
32 devices in a mesh: grp: 4 (over z), tile: 8 (over y, x, core).
Axes of the slice: x: 2, y: 2, z: 4, core: 2. Of those that a mesh axis runs over, the one named last changes fastest.
Arguments:
- speed: float32 [32, 2, 32, 128], P('tile'), may hold values from 0.15 to 0.4
- density: float32 [32, 2, 32, 128], P('tile'), may hold values from 1 to 3
- fwd_state: bfloat16 [32, 4, 8, 32, 128], P(('grp', 'tile')), may hold values from -6 to 6
- adj_state: bfloat16 [32, 4, 8, 32, 128], P(('grp', 'tile')), may hold values from -6 to 6
- aperture: int32 [32, 4], P(('grp', 'tile')), may hold values from 0 to 31, as said below
- src_pos: int32 [32, 3], P(('grp', 'tile')), may hold values from 0 to 127, as said below
- wavelet: float32 [32, 4], P(('grp', 'tile')), may hold values from -15 to 15
- rec_pos: int32 [32, 8, 2], P(('grp', 'tile')), may hold values from 0 to 127, as said below
- residual: float32 [32, 4, 8], P(('grp', 'tile')), may hold values from -6 to 6
Outputs:
- grad_speed: float32 [32, 2, 32, 128], P('tile')
- grad_density: float32 [32, 2, 32, 128], P('tile')
Inputs may be any that keep to these rules, and one draw needn't show every extreme that they name: `aperture`: row s is (c + j) * 4 + e for j = 0 .. 3, with one c in 0 .. 4 and one e in 0 .. 3 for each shot, so a shot takes exactly one tile from each of 4 owners. `src_pos`: columns are x in 0 .. 7, y in 0 .. 31, z in 0 .. 127. `rec_pos`: columns are y in 0 .. 31 and z in 0 .. 127.
All inputs are finite; a program needn't handle non-finite values.
Results may differ from a plain program's by a relative error of at most 0.0003.
Values sent between devices are 32-bit elements; how exact they have to be, the bound alone decides.
No kernel may reach another device: no remote copies, remote signals or barrier semaphores. Data moves between devices by JAX's collectives and lax.ppermute only.
A program may use at most 64 MiB of HBM per device.

v0:
```python
import functools
import math

import jax
import jax.numpy as jnp
from jax import lax
from jax.experimental import pallas as pl
from jax.experimental.pallas import tpu as pltpu
from jax.sharding import PartitionSpec as P

COEF = (1225.0 / 1024.0, -245.0 / 3072.0, 49.0 / 5120.0, -5.0 / 7168.0)
REACH = 4
EDGE = 8
ROWS = 8
SPAN = 8

SMEM = pl.BlockSpec(memory_space=pltpu.SMEM)
VMEM = pl.BlockSpec(memory_space=pltpu.VMEM)
PARAMS = pltpu.CompilerParams(vmem_limit_bytes=36 * 1024 * 1024)


def entry_of(list_ref):
    return jnp.max(list_ref[0:1, 0:1].astype(jnp.float32)).astype(jnp.int32)


def combine(ahead, behind):
    total = None
    for order in range(1, 5):
        upper, lower = ahead(order), behind(order)
        if upper is None and lower is None:
            continue
        if lower is None:
            term = upper
        elif upper is None:
            term = -lower
        else:
            term = upper - lower
        if order > 1:
            term = (COEF[order - 1] / COEF[0]) * term
        total = term if total is None else total + term
    return total


def band(first, depth):
    source = lax.broadcasted_iota(jnp.int32, (depth, depth), 0)
    target = lax.broadcasted_iota(jnp.int32, (depth, depth), 1)
    total = jnp.zeros((depth, depth), jnp.float32)
    for order in range(1, 5):
        weight = COEF[order - 1] / COEF[0]
        total = total + jnp.where(source == target + (first + order - 1), weight, 0.0)
        total = total - jnp.where(source == target + (first - order), weight, 0.0)
    return jnp.concatenate(halves(total), axis=1)


def halves(values):
    high = values.astype(jnp.bfloat16)
    return high, (values - high.astype(jnp.float32)).astype(jnp.bfloat16)


def along_z(values, matrix):
    xs, ys, zs = values.shape
    pair = jnp.concatenate(halves(values.reshape(xs * ys, zs)), axis=1)
    parts = jnp.dot(pair, matrix, preferred_element_type=jnp.float32)
    return (parts[:, :zs] + parts[:, zs:]).reshape(xs, ys, zs)


def blocks(xs, ys, body):
    if xs <= SPAN:
        for y0 in range(0, ys, ROWS):
            body(0, xs, y0)
        return

    def span(index, _):
        for y0 in range(0, ys, ROWS):
            body(index * SPAN, SPAN, y0)
        return 0

    lax.fori_loop(0, xs // SPAN, span, 0)


def window(xs, x0, load):
    kept = {}

    def at(offset):
        if xs <= SPAN and not 0 <= offset < xs:
            return None
        if offset not in kept:
            kept[offset] = load(x0 + offset)
        return kept[offset]

    return at


def slopes(xs, p, x0, y0, plane, offset):
    centre = plane(offset)
    here = x0 + offset + REACH
    return (
        combine(lambda k: plane(offset + k), lambda k: plane(offset + 1 - k)),
        combine(
            lambda k: p[here, pl.ds(EDGE + y0 + k, ROWS)],
            lambda k: centre if k == 1 else p[here, pl.ds(EDGE + y0 + 1 - k, ROWS)],
        ),
    )


def prepare_kernel(
    steps, fwd, adj, src, wave, rec, res, _piece,
    fwd_slope, adj_slope, fwd_source, adj_source, ahead, behind, *fields,
):
    xs, ys, zs = fwd_slope.shape[1:]
    for ref, first in ((ahead, 1), (behind, 0)):
        one = band(first, zs)
        ref[:zs] = one
        ref[zs:] = one

    def clear(ref):
        ref[...] = jnp.zeros(ref.shape, jnp.float32)

    for state, (p, v0, v1, v2), slope in (
        (fwd, fields[:4], fwd_slope),
        (adj, fields[4:], adj_slope),
    ):
        for ref in (p, v0):
            clear(ref.at[:REACH])
            clear(ref.at[REACH + xs :])
        for ref in (p.at[pl.ds(REACH, xs)], v1):
            clear(ref.at[:, :EDGE])
            clear(ref.at[:, EDGE + ys :])
        for x in range(xs):
            p[REACH + x, EDGE : EDGE + ys] = state[0, 0, x].astype(jnp.float32)
            v0[REACH + x] = state[0, 1, x].astype(jnp.float32)
            v1[x, EDGE : EDGE + ys] = state[0, 2, x].astype(jnp.float32)
            v2[x] = state[0, 3, x].astype(jnp.float32)

        def block(x0, count, y0, p=p, slope=slope):
            plane = window(xs, x0, lambda x: p[REACH + x, pl.ds(EDGE + y0, ROWS)])
            for offset in range(count):
                for d, values in enumerate(slopes(xs, p, x0, y0, plane, offset)):
                    slope[d, x0 + offset, pl.ds(y0, ROWS)] = values

        blocks(xs, ys, block)
        slope[2] = along_z(p[REACH : REACH + xs, EDGE : EDGE + ys], ahead[...])

    row = lax.broadcasted_iota(jnp.int32, (ys, zs), 0)
    lane = lax.broadcasted_iota(jnp.int32, (ys, zs), 1)
    src_mark = (row == src[0, 1]) & (lane == src[0, 2])
    for x in range(xs):
        rec_mark = (row == rec[0, 0, x]) & (lane == rec[0, 1, x])
        for step in range(steps):
            amplitude = jnp.where(x == src[0, 0], wave[0, step], 0.0)
            fwd_source[step, x] = jnp.where(src_mark, amplitude, 0.0)
            adj_source[step, x] = jnp.where(rec_mark, res[0, step, x], 0.0)


def near_kernel(speed, density, aperture, near_speed, near_density, entry):
    near_speed[...] = speed[...]
    near_density[...] = density[...]
    entry[...] = jnp.full(entry.shape, entry_of(aperture), jnp.int32)


def pick_kernel(chips, near_speed, near_density, far_speed, far_density, *refs):
    stripes = 2 * chips
    lists, outs = refs[:stripes], refs[stripes:]
    held = near_speed.shape[0]
    me = lax.axis_index("tile")
    residue, half = lax.rem(me, stripes), lax.div(me, stripes)
    for hop in range(stripes):
        entry = entry_of(lists[hop])
        corner, column = lax.div(entry, held), lax.rem(entry, held)
        here = (residue >= corner) == (half == 0)
        piece = outs[hop]

        @pl.when(here)
        def _():
            piece[0] = near_speed[column]
            piece[1] = near_density[column]

        @pl.when(jnp.logical_not(here))
        def _():
            piece[0] = far_speed[column]
            piece[1] = far_density[column]


def wave_kernel(chips, steps, held, *refs):
    stripes = 2 * chips
    pieces, refs = refs[:stripes], refs[stripes:]
    fwd_slope, adj_slope, fwd_source, adj_source, ahead, behind, entry_ref = refs[:7]
    kept, traded, p, v0, v1, v2, q, w0, w1, w2 = refs[15:25]
    bulk, buoy, dp, dv, bulk_img, buoy_img, across_z, flat = refs[25:]
    tile_x, tile_y = pieces[0].shape[1:3]
    xs, ys, zs = bulk.shape
    residue = lax.rem(lax.axis_index("tile"), stripes)
    entry = entry_of(entry_ref)
    corner = lax.div(entry, held)

    def place_of(hop):
        return lax.rem((residue ^ hop) - corner + stripes, stripes) * tile_x

    for hop in range(stripes):
        cells = pl.ds(place_of(hop), tile_x)
        speed, density = pieces[hop][0], pieces[hop][1]
        bulk[cells] = COEF[0] * (density * speed * speed)
        buoy[cells] = COEF[0] / density

    def push(fields, first, note):
        p, v0, v1, v2 = fields
        if first is None:
            across_z[...] = along_z(p[REACH : REACH + xs, EDGE : EDGE + ys], ahead[...])

        def block(x0, count, y0):
            rows, inner = pl.ds(y0, ROWS), pl.ds(EDGE + y0, ROWS)
            plane = window(xs, x0, lambda x: p[REACH + x, inner])
            for offset in range(count):
                x = x0 + offset
                if first is None:
                    two = slopes(xs, p, x0, y0, plane, offset)
                else:
                    two = (first[0, x, rows], first[1, x, rows])
                places = ((v0, REACH + x, rows), (v1, x, inner))
                for d, (ref, at, span) in enumerate(places):
                    change = buoy[x, rows] * two[d]
                    moved = ref[at, span] + change
                    ref[at, span] = moved
                    note(d, x, rows, change, moved)

        def block_z(x0, count, y0):
            rows = pl.ds(y0, ROWS)
            for x in range(count):
                x = x0 + x
                slope = across_z[x, rows] if first is None else first[2, x, rows]
                change = buoy[x, rows] * slope
                moved = v2[x, rows] + change
                v2[x, rows] = moved
                note(2, x, rows, change, moved)

        blocks(xs, ys, block)
        blocks(xs, ys, block_z)

    def spread(fields, source, step, note):
        p, v0, v1, v2 = fields
        across_z[...] = along_z(v2[...], behind[...])

        def block(x0, count, y0):
            rows = pl.ds(y0, ROWS)
            plane = window(xs, x0, lambda x: v0[REACH + x, rows])
            for offset in range(count):
                x = x0 + offset
                along_x = combine(lambda k: plane(offset + k - 1), lambda k: plane(offset - k))
                along_y = combine(
                    lambda k: v1[x, pl.ds(EDGE + y0 + k - 1, ROWS)],
                    lambda k: v1[x, pl.ds(EDGE + y0 - k, ROWS)],
                )
                flat[x, rows] = along_x + along_y

        def block_z(x0, count, y0):
            rows, inner = pl.ds(y0, ROWS), pl.ds(EDGE + y0, ROWS)
            for x in range(count):
                x = x0 + x
                change = bulk[x, rows] * (flat[x, rows] + across_z[x, rows])
                change = change + source[step, x, rows]
                moved = p[REACH + x, inner] + change
                p[REACH + x, inner] = moved
                note(x, rows, change, moved)

        blocks(xs, ys, block)
        blocks(xs, ys, block_z)

    fields = (p, v0, v1, v2)
    for step in range(steps):

        def keep_dv(d, x, rows, change, moved, step=step):
            dv[step, d, x, rows] = change

        def keep_dp(x, rows, change, moved, step=step):
            dp[step, x, rows] = change

        push(fields, fwd_slope if step == 0 else None, keep_dv)
        spread(fields, fwd_source, step, keep_dp)

    fields = (q, w0, w1, w2)
    for step in reversed(range(steps)):
        last = step == steps - 1

        def add_buoy(d, x, rows, change, moved, step=step, last=last):
            image = dv[step, d, x, rows] * moved
            buoy_img[x, rows] = image if last and d == 0 else buoy_img[x, rows] + image

        def add_bulk(x, rows, change, moved, step=step, last=last):
            image = dp[step, x, rows] * moved
            bulk_img[x, rows] = image if last else bulk_img[x, rows] + image

        push(fields, adj_slope if last else None, add_buoy)
        spread(fields, adj_source, step, add_bulk)

    tile_rows = tile_x * tile_y
    for chip in range(chips):
        for ref, hop in ((kept, 2 * chip), (traded, 2 * chip + 1)):
            cells = pl.ds(place_of(hop), tile_x)
            ref[chip, :tile_rows] = bulk_img[cells].reshape(tile_rows, zs)
            ref[chip, tile_rows : 2 * tile_rows] = buoy_img[cells].reshape(tile_rows, zs)
            ref[chip, 2 * tile_rows :] = jnp.full((8, zs), entry).astype(jnp.float32)


def merge_kernel(chips, kept, came, *outs):
    tile_rows = (kept.shape[1] - 8) // 2
    half = lax.div(lax.axis_index("tile"), 2 * chips)
    for index, out in enumerate(outs):
        chip, other = index % chips, index // chips
        field = jnp.where(half == other, 0, 1)
        rows = pl.ds(pl.multiple_of(field * tile_rows, tile_rows), tile_rows)
        for shot, source in enumerate((kept, came)):
            out[shot * tile_rows : (shot + 1) * tile_rows] = source[chip, rows]
            first = 2 * tile_rows + 4 * shot
            out[first : first + 4] = source[chip, 2 * tile_rows : 2 * tile_rows + 4]


def add_kernel(stripes, groups, held, *refs):
    came, parts, total = refs[:stripes], refs[stripes:-1], refs[-1]
    me, group = lax.axis_index("tile"), lax.axis_index("grp")
    residue, half = lax.rem(me, stripes), lax.div(me, stripes)
    tile_rows = total.shape[0] // (2 * held)
    part = parts[0].shape[0]
    total[...] = jnp.zeros_like(total)
    for pair in came:
        for shot in range(2):
            first = 2 * tile_rows + 4 * shot
            entry = jnp.max(pair[first : first + 4]).astype(jnp.int32)
            corner, column = lax.div(entry, held), lax.rem(entry, held)
            slot = jnp.where(residue < corner, held, 0) + column
            rows = pl.ds(pl.multiple_of(slot * tile_rows, tile_rows), tile_rows)
            total[rows] = total[rows] + pair[shot * tile_rows : (shot + 1) * tile_rows]
    for out, (hop, flip) in zip(parts, part_order(groups)):
        owner = jnp.where(half == flip, 0, 1)
        first = owner * (held * tile_rows) + (group ^ hop) * part
        out[...] = total[pl.ds(pl.multiple_of(first, part), part)]


def part_order(groups):
    hops = [(hop, flip) for hop in far_first(groups) for flip in range(2)]
    return [(0, 0)] + hops + [(0, 1)]


def far_first(groups):
    return list(range(groups - 1, 0, -1))


def grads_kernel(scale, groups, stripes, *refs):
    parts, speed_ref, density_ref, grads = refs[: 2 * groups], *refs[2 * groups :]
    part = parts[0].shape[0]
    rows = pl.ds(pl.multiple_of(lax.axis_index("grp") * part, part), part)
    speed, density = speed_ref[rows], density_ref[rows]
    sums = [None, None]
    for values, (_, flip) in zip(parts, part_order(groups)):
        sums[flip] = values[...] if sums[flip] is None else sums[flip] + values[...]
    first_half = lax.axis_index("tile") < stripes
    bulk_sum = jnp.where(first_half, sums[0], sums[1])
    buoy_sum = jnp.where(first_half, sums[1], sums[0])
    grads[0] = scale * (bulk_sum * (2.0 * density * speed))
    grads[1] = scale * (bulk_sum * (speed * speed) - buoy_sum / (density * density))


def per_device(speed, density, fwd_state, adj_state, aperture, src_pos, wavelet, rec_pos, residual):
    owners = lax.axis_size("tile")
    groups = lax.axis_size("grp")
    my_group = lax.axis_index("grp")
    held, tile_x, tile_y, depth = speed.shape
    stripes = aperture.shape[1]
    chips = stripes // 2
    steps = wavelet.shape[1]
    xs = stripes * tile_x
    f32 = jnp.float32
    cells = (xs, tile_y, depth)

    def shape(*dims):
        return jax.ShapeDtypeStruct(dims, f32)

    def across(values, hop):
        return lax.ppermute(values, "tile", [(t, t ^ hop) for t in range(owners)])

    far_speed = across(speed, stripes)
    far_density = across(density, stripes)
    lists = {hop: across(aperture, hop) for hop in range(stripes - 1, 0, -1)}
    four = [
        (xs + 2 * REACH, tile_y + 2 * EDGE, depth),
        (xs + 2 * REACH, tile_y, depth),
        (xs, tile_y + 2 * EDGE, depth),
        cells,
    ]
    near_speed, near_density, entry = pl.pallas_call(
        near_kernel,
        out_shape=[
            shape(*speed.shape),
            shape(*speed.shape),
            jax.ShapeDtypeStruct((8, depth), jnp.int32),
        ],
        in_specs=[VMEM] * 3,
        out_specs=[VMEM] * 3,
        compiler_params=PARAMS,
        cost_estimate=pl.CostEstimate(flops=4_000_000, bytes_accessed=6_000_000, transcendentals=0),
        name="hold_near_tiles",
    )(speed, density, aperture)
    pieces = pl.pallas_call(
        functools.partial(pick_kernel, chips),
        out_shape=[shape(2, tile_x, tile_y, depth)] * stripes,
        in_specs=[VMEM] * (4 + stripes),
        out_specs=[VMEM] * stripes,
        compiler_params=PARAMS,
        name="pick_tiles",
    )(near_speed, near_density, far_speed, far_density, entry, *[lists[h] for h in range(1, stripes)])
    moved = {hop: across(pieces[hop], hop) for hop in range(stripes - 1, 0, -1)}

    prepared = pl.pallas_call(
        functools.partial(prepare_kernel, steps),
        out_shape=[shape(3, *cells)] * 2
        + [shape(steps, *cells)] * 2
        + [jax.ShapeDtypeStruct((2 * depth, 2 * depth), jnp.bfloat16)] * 2
        + [shape(*dims) for dims in four + four],
        in_specs=[VMEM] * 2 + [SMEM] * 4 + [VMEM],
        out_specs=[VMEM] * 14,
        compiler_params=PARAMS,
        cost_estimate=pl.CostEstimate(flops=4_000_000, bytes_accessed=6_000_000, transcendentals=0),
        name="prepare",
    )(fwd_state, adj_state, src_pos, wavelet, jnp.swapaxes(rec_pos, 1, 2), residual, pieces[0])
    prepared, fields = prepared[:6], prepared[6:]
    pieces = [pieces[0]] + [moved[hop] for hop in range(1, stripes)]

    tile_rows = tile_x * tile_y
    sent = shape(chips, 2 * tile_rows + 8, depth)
    kept, traded, *_ = pl.pallas_call(
        functools.partial(wave_kernel, chips, steps, held),
        out_shape=[sent, sent] + [shape(*dims) for dims in four + four],
        in_specs=[VMEM] * (stripes + 15),
        out_specs=[VMEM] * 10,
        scratch_shapes=[
            pltpu.VMEM(cells, f32),
            pltpu.VMEM(cells, f32),
            pltpu.VMEM((steps,) + cells, f32),
            pltpu.VMEM((steps, 3) + cells, f32),
            pltpu.VMEM(cells, f32),
            pltpu.VMEM(cells, f32),
            pltpu.VMEM(cells, f32),
            pltpu.VMEM(cells, f32),
        ],
        input_output_aliases={stripes + 7 + index: 2 + index for index in range(8)},
        compiler_params=PARAMS,
        name="replay_and_adjoint",
    )(*pieces, *prepared, entry, *fields)

    stacks = pl.pallas_call(
        functools.partial(merge_kernel, chips),
        out_shape=[shape(2 * tile_rows + 8, depth)] * stripes,
        in_specs=[VMEM] * 2,
        out_specs=[VMEM] * stripes,
        compiler_params=PARAMS,
        name="merge_pair",
    )(kept, across(traded, 1))
    came = [across(stacks[chip], 2 * chip) if chip else stacks[0] for chip in range(stripes)]

    rows = held * tile_rows
    part = rows // groups
    parts = pl.pallas_call(
        functools.partial(add_kernel, stripes, groups, held),
        out_shape=[shape(part, depth)] * (2 * groups),
        in_specs=[VMEM] * stripes,
        out_specs=[VMEM] * (2 * groups),
        scratch_shapes=[pltpu.VMEM((2 * rows, depth), f32)],
        compiler_params=PARAMS,
        name="add_stripes",
    )(*came)

    def along(values, hop, flip=0):
        pairs = [
            (g * owners + t, (g ^ hop) * owners + (t ^ (flip * stripes)))
            for g in range(groups)
            for t in range(owners)
        ]
        return lax.ppermute(values, ("grp", "tile"), pairs)

    parts = [
        along(values, *hops) if any(hops) else values
        for values, hops in zip(parts, part_order(groups))
    ]
    grads = pl.pallas_call(
        functools.partial(grads_kernel, 1.0 / math.sqrt(groups * owners), groups, stripes),
        out_shape=shape(2, part, depth),
        in_specs=[VMEM] * (2 * groups + 2),
        out_specs=VMEM,
        compiler_params=PARAMS,
        name="gradients",
    )(*parts, near_speed.reshape(rows, depth), near_density.reshape(rows, depth))

    whole = jnp.zeros((2, groups, part, depth), f32)
    for hop in [0] + far_first(groups):
        values = grads if hop == 0 else along(grads, hop)
        place = my_group ^ hop
        whole = lax.dynamic_update_slice_in_dim(whole, values[:, None], place, axis=1)
    return (whole[0].reshape(speed.shape), whole[1].reshape(speed.shape))


def solution(mesh):
    return jax.shard_map(
        per_device,
        mesh=mesh,
        in_specs=(
            P("tile", None, None, None),
            P("tile", None, None, None),
            P(("grp", "tile"), None, None, None, None),
            P(("grp", "tile"), None, None, None, None),
            P(("grp", "tile"), None),
            P(("grp", "tile"), None),
            P(("grp", "tile"), None),
            P(("grp", "tile"), None, None),
            P(("grp", "tile"), None, None),
        ),
        out_specs=(P("tile", None, None, None), P("tile", None, None, None)),
        check_vma=False,
    )
```

profile of v0, /device:TPU:0, one launch (start us, length us, event | category | flops | bytes accessed | tf_op | source)
XLA Modules:
  0.0 51.9 jit_solution(3614333321670623758)
XLA Ops:
  0.6 3.0 %collective-permute-start = (f32[4,2,32,128]{3,2,1,0:T(8,128)}, f32[4,2,32,128]{3,2,1,0:T(8,128)S(1)}, u32[]{:S(2)}, u32[]{:S(2)}) collective-permute-start(f32[4,2,32,128]{3,2,1,0:T(8,128)} %speed.1), channel_id=1, source_target_pairs={{0,4},{1,5},{2,6},{3,7},{4,0},{5,1},{6,2},{7,3},{8,12},{9,13},{10,... | collective-permute-start | bytes 393224 | tf_op jit(solution)/shard_map/ppermute | solution.py:378
  3.7 0.1 collective-permute-start.1
  3.7 0.0 collective-permute-start.2
  3.7 1.9 %collective-permute-start.3 = (s32[1,4]{1,0:T(1,128)}, s32[1,4]{1,0:T(1,128)S(1)}, u32[]{:S(2)}, u32[]{:S(2)}) collective-permute-start(s32[1,4]{1,0:T(1,128)} %aperture.1), channel_id=1, source_target_pairs={{0,2},{1,3},{2,0},{3,1},{4,6},{5,7},{6,4},{7,5},{8,10},{9,11},{10,... | collective-permute-start | bytes 56 | tf_op jit(solution)/shard_map/ppermute | solution.py:378
  5.7 0.2 collective-permute-start.4
  5.8 0.0 copy-start.2
  5.8 0.9 %copy-done.2 = f32[4,2,32,128]{3,2,1,0:T(8,128)S(1)} copy-done((f32[4,2,32,128]{3,2,1,0:T(8,128)S(1)}, f32[4,2,32,128]{3,2,1,0:T(8,128)}, u32[]{:S(2)}) %copy-start.2) | copy-done | bytes 131096
  6.7 0.0 copy-start.3
  6.7 0.9 %copy-done.3 = f32[4,2,32,128]{3,2,1,0:T(8,128)S(1)} copy-done((f32[4,2,32,128]{3,2,1,0:T(8,128)S(1)}, f32[4,2,32,128]{3,2,1,0:T(8,128)}, u32[]{:S(2)}) %copy-start.3) | copy-done | bytes 131096
  7.6 0.0 copy-start.6
  7.6 0.7 %copy-done.6 = s32[1,4]{1,0:T(1,128)S(1)} copy-done((s32[1,4]{1,0:T(1,128)S(1)}, s32[1,4]{1,0:T(1,128)}, u32[]{:S(2)}) %copy-start.6) | copy-done | bytes 40
  8.3 0.1 hold_near_tiles.1
  8.4 0.0 collective-permute-done.2.refs_1_
  8.4 0.0 collective-permute-done.3.refs_2_
  8.4 0.4 collective-permute-done.4.refs_3_
  8.8 0.0 collective-permute-done.far_speed
  8.8 1.4 %collective-permute-done.1.far_density = f32[4,2,32,128]{3,2,1,0:T(8,128)S(1)} collective-permute-done((f32[4,2,32,128]{3,2,1,0:T(8,128)}, f32[4,2,32,128]{3,2,1,0:T(8,128)S(1)}, u32[]{:S(2)}, u32[]{:S(2)}) %collective-permute-start.1) | collective-permute-done | bytes 131104 | tf_op jit(solution)/shard_map/ppermute | solution.py:378
  10.2 0.0 copy-start
  10.2 0.0 copy-start.8
  10.2 0.2 pick_tiles.1
  10.4 0.1 collective-permute-start.5
  10.5 1.8 %collective-permute-start.6 = (f32[2,2,32,128]{3,2,1,0:T(8,128)S(1)}, f32[2,2,32,128]{3,2,1,0:T(8,128)S(1)}, u32[]{:S(2)}, u32[]{:S(2)}) collective-permute-start(f32[2,2,32,128]{3,2,1,0:T(8,128)S(1)} %get-tuple-element.42), channel_id=1, source_target_pairs={{0,2},{1,3},{2,0},{3,1},{4,6},{5,7},{6,4},{7,5},{8,10},{9,11},{10,... | collective-permute-start | bytes 196616 | tf_op jit(solution)/shard_map/ppermute | solution.py:378
  12.3 0.1 collective-permute-start.7
  12.3 0.0 copy-done
  12.4 0.0 copy-done.1
  12.4 0.0 copy-done.8
  12.4 0.6 %copy-done.4 = f32[1,4,8]{2,1,0:T(4,128)S(1)} copy-done((f32[1,4,8]{2,1,0:T(4,128)S(1)}, f32[1,4,8]{2,1,0:T(4,128)}, u32[]{:S(2)}) %copy-start.4) | copy-done | bytes 152
  12.9 0.1 copy-done.5
  13.0 0.0 copy-done.7
  13.0 1.3 %prepare.1 = (f32[3,8,32,128]{3,2,1,0:T(8,128)S(1)}, f32[3,8,32,128]{3,2,1,0:T(8,128)S(1)}, f32[4,8,32,128]{3,2,1,0:T(8,128)S(1)}, f32[4,8,32,128]{3,2,1,0:T(8,1...) custom-call(bf16[1,4,8,32,128]{4,3,2,1,0:T(8,128)(2,1)S(1)} %copy-do, ...), custom_call_target="tpu_custom_call" | custom-call | flops 4000000 | bytes 6000000 | tf_op jit(solution)/shard_map/prepare/pallas_call | solution.py:412
  14.3 0.0 collective-permute-done.5.refs_1_
  14.3 0.7 %collective-permute-done.6.refs_2_ = f32[2,2,32,128]{3,2,1,0:T(8,128)S(1)} collective-permute-done((f32[2,2,32,128]{3,2,1,0:T(8,128)S(1)}, f32[2,2,32,128]{3,2,1,0:T(8,128)S(1)}, u32[]{:S(2)}, u32[]{:S(2)}) %collective-permute-start.6) | collective-permute-done | bytes 65568 | tf_op jit(solution)/shard_map/ppermute | solution.py:378
  15.0 1.3 %collective-permute-done.7.refs_3_ = f32[2,2,32,128]{3,2,1,0:T(8,128)S(1)} collective-permute-done((f32[2,2,32,128]{3,2,1,0:T(8,128)S(1)}, f32[2,2,32,128]{3,2,1,0:T(8,128)S(1)}, u32[]{:S(2)}, u32[]{:S(2)}) %collective-permute-start.7) | collective-permute-done | bytes 65568 | tf_op jit(solution)/shard_map/ppermute | solution.py:378
  16.3 2.3 %replay_and_adjoint.1 = (f32[2,136,128]{2,1,0:T(8,128)S(1)}, f32[2,136,128]{2,1,0:T(8,128)S(1)}, f32[16,48,128]{2,1,0:T(8,128)S(1)}, f32[16,32,128]{2,1,0:T(8,12...) custom-call(f32[2,2,32,128]{3,2,1,0:T(8,128)S(1)} %get-tuple-element, ...), custom_call_target="tpu_custom_call", output_to_operand_aliasing={{2}: (11, {}), {3}: (12, {}), {4}: (13, {}), {5}: (14, {}),... | custom-call | tf_op jit(solution)/shard_map/replay_and_adjoint/pallas_call | solution.py:429
  18.7 0.2 collective-permute-start.8
  18.9 1.2 %collective-permute-done.8.came = f32[2,136,128]{2,1,0:T(8,128)S(1)} collective-permute-done((f32[2,136,128]{2,1,0:T(8,128)S(1)}, f32[2,136,128]{2,1,0:T(8,128)S(1)}, u32[]{:S(2)}, u32[]{:S(2)}) %collective-permute-start.8) | collective-permute-done | bytes 139296 | tf_op jit(solution)/shard_map/ppermute | solution.py:378
  20.1 1.6 %collective-permute-start.10 = (f32[136,128]{1,0:T(8,128)S(1)}, f32[136,128]{1,0:T(8,128)S(1)}, u32[]{:S(2)}, u32[]{:S(2)}) collective-permute-start(f32[136,128]{1,0:T(8,128)S(1)} %get-tuple-element.62), channel_id=1, source_target_pairs={{0,4},{1,5},{2,6},{3,7},{4,0},{5,1},{6,2},{7,3},{8,12},{9,13},{10,... | collective-permute-start | bytes 208904 | tf_op jit(solution)/shard_map/ppermute | solution.py:378
  21.7 1.3 %collective-permute-start.11 = (f32[136,128]{1,0:T(8,128)S(1)}, f32[136,128]{1,0:T(8,128)S(1)}, u32[]{:S(2)}, u32[]{:S(2)}) collective-permute-start(f32[136,128]{1,0:T(8,128)S(1)} %get-tuple-element.63), channel_id=1, source_target_pairs={{0,6},{1,7},{2,4},{3,5},{4,2},{5,3},{6,0},{7,1},{8,14},{9,15},{10,... | collective-permute-start | bytes 208904 | tf_op jit(solution)/shard_map/ppermute | solution.py:378
  23.0 0.7 %collective-permute-start.9 = (f32[136,128]{1,0:T(8,128)S(1)}, f32[136,128]{1,0:T(8,128)S(1)}, u32[]{:S(2)}, u32[]{:S(2)}) collective-permute-start(f32[136,128]{1,0:T(8,128)S(1)} %get-tuple-element.61), channel_id=1, source_target_pairs={{0,2},{1,3},{2,0},{3,1},{4,6},{5,7},{6,4},{7,5},{8,10},{9,11},{10,... | collective-permute-start | bytes 208904 | tf_op jit(solution)/shard_map/ppermute | solution.py:378
  23.7 0.8 %collective-permute-done.10.refs_2_ = f32[136,128]{1,0:T(8,128)S(1)} collective-permute-done((f32[136,128]{1,0:T(8,128)S(1)}, f32[136,128]{1,0:T(8,128)S(1)}, u32[]{:S(2)}, u32[]{:S(2)}) %collective-permute-start.10) | collective-permute-done | bytes 69664 | tf_op jit(solution)/shard_map/ppermute | solution.py:378
  24.5 3.1 %collective-permute-done.11.refs_3_ = f32[136,128]{1,0:T(8,128)S(1)} collective-permute-done((f32[136,128]{1,0:T(8,128)S(1)}, f32[136,128]{1,0:T(8,128)S(1)}, u32[]{:S(2)}, u32[]{:S(2)}) %collective-permute-start.11) | collective-permute-done | bytes 69664 | tf_op jit(solution)/shard_map/ppermute | solution.py:378
  27.6 0.0 collective-permute-done.9.refs_1_
  27.6 0.2 add_stripes.1
  27.8 3.7 %collective-permute-start.12 = (f32[64,128]{1,0:T(8,128)S(1)}, f32[64,128]{1,0:T(8,128)S(1)}, u32[]{:S(2)}, u32[]{:S(2)}) collective-permute-start(f32[64,128]{1,0:T(8,128)S(1)} %get-tuple-element.65), channel_id=1, source_target_pairs={{0,24},{1,25},{2,26},{3,27},{4,28},{5,29},{6,30},{7,31},{8,16},{9,... | collective-permute-start | bytes 98312 | tf_op jit(solution)/shard_map/ppermute | solution.py:477
  31.4 1.1 %collective-permute-start.13 = (f32[64,128]{1,0:T(8,128)S(1)}, f32[64,128]{1,0:T(8,128)S(1)}, u32[]{:S(2)}, u32[]{:S(2)}) collective-permute-start(f32[64,128]{1,0:T(8,128)S(1)} %get-tuple-element.66), channel_id=1, source_target_pairs={{0,28},{1,29},{2,30},{3,31},{4,24},{5,25},{6,26},{7,27},{8,20},{9,... | collective-permute-start | bytes 98312 | tf_op jit(solution)/shard_map/ppermute | solution.py:477
  32.5 0.8 %collective-permute-start.14 = (f32[64,128]{1,0:T(8,128)S(1)}, f32[64,128]{1,0:T(8,128)S(1)}, u32[]{:S(2)}, u32[]{:S(2)}) collective-permute-start(f32[64,128]{1,0:T(8,128)S(1)} %get-tuple-element.67), channel_id=1, source_target_pairs={{0,16},{1,17},{2,18},{3,19},{4,20},{5,21},{6,22},{7,23},{8,24},{9,... | collective-permute-start | bytes 98312 | tf_op jit(solution)/shard_map/ppermute | solution.py:477
  33.3 2.2 %collective-permute-start.15 = (f32[64,128]{1,0:T(8,128)S(1)}, f32[64,128]{1,0:T(8,128)S(1)}, u32[]{:S(2)}, u32[]{:S(2)}) collective-permute-start(f32[64,128]{1,0:T(8,128)S(1)} %get-tuple-element.68), channel_id=1, source_target_pairs={{0,20},{1,21},{2,22},{3,23},{4,16},{5,17},{6,18},{7,19},{8,28},{9,... | collective-permute-start | bytes 98312 | tf_op jit(solution)/shard_map/ppermute | solution.py:477
  35.5 1.2 %collective-permute-start.16 = (f32[64,128]{1,0:T(8,128)S(1)}, f32[64,128]{1,0:T(8,128)S(1)}, u32[]{:S(2)}, u32[]{:S(2)}) collective-permute-start(f32[64,128]{1,0:T(8,128)S(1)} %get-tuple-element.69), channel_id=1, source_target_pairs={{0,8},{1,9},{2,10},{3,11},{4,12},{5,13},{6,14},{7,15},{8,0},{9,1},... | collective-permute-start | bytes 98312 | tf_op jit(solution)/shard_map/ppermute | solution.py:477
  36.7 0.0 collective-permute-done.12.refs_1_
  36.7 1.6 %collective-permute-start.17 = (f32[64,128]{1,0:T(8,128)S(1)}, f32[64,128]{1,0:T(8,128)S(1)}, u32[]{:S(2)}, u32[]{:S(2)}) collective-permute-start(f32[64,128]{1,0:T(8,128)S(1)} %get-tuple-element.70), channel_id=1, source_target_pairs={{0,12},{1,13},{2,14},{3,15},{4,8},{5,9},{6,10},{7,11},{8,4},{9,5},... | collective-permute-start | bytes 98312 | tf_op jit(solution)/shard_map/ppermute | solution.py:477
  38.3 0.0 collective-permute-done.13.refs_2_
  38.3 1.1 %collective-permute-start.18 = (f32[64,128]{1,0:T(8,128)S(1)}, f32[64,128]{1,0:T(8,128)S(1)}, u32[]{:S(2)}, u32[]{:S(2)}) collective-permute-start(f32[64,128]{1,0:T(8,128)S(1)} %get-tuple-element.71), channel_id=1, source_target_pairs={{0,4},{1,5},{2,6},{3,7},{4,0},{5,1},{6,2},{7,3},{8,12},{9,13},{10,... | collective-permute-start | bytes 98312 | tf_op jit(solution)/shard_map/ppermute | solution.py:477
  39.5 0.0 collective-permute-done.14.refs_3_
  39.5 0.0 collective-permute-done.15.refs_4_
  39.5 0.0 collective-permute-done.16.refs_5_
  39.5 2.1 %collective-permute-done.17.refs_6_ = f32[64,128]{1,0:T(8,128)S(1)} collective-permute-done((f32[64,128]{1,0:T(8,128)S(1)}, f32[64,128]{1,0:T(8,128)S(1)}, u32[]{:S(2)}, u32[]{:S(2)}) %collective-permute-start.17) | collective-permute-done | bytes 32800 | tf_op jit(solution)/shard_map/ppermute | solution.py:477
  41.5 0.7 %collective-permute-done.18.refs_7_ = f32[64,128]{1,0:T(8,128)S(1)} collective-permute-done((f32[64,128]{1,0:T(8,128)S(1)}, f32[64,128]{1,0:T(8,128)S(1)}, u32[]{:S(2)}, u32[]{:S(2)}) %collective-permute-start.18) | collective-permute-done | bytes 32800 | tf_op jit(solution)/shard_map/ppermute | solution.py:477
  42.3 3.7 %collective-permute-start.19 = (f32[2,64,128]{2,1,0:T(8,128)S(1)}, f32[2,64,128]{2,1,0:T(8,128)S(1)}, u32[]{:S(2)}, u32[]{:S(2)}) collective-permute-start(f32[2,64,128]{2,1,0:T(8,128)S(1)} %gradients.1), channel_id=1, source_target_pairs={{0,24},{1,25},{2,26},{3,27},{4,28},{5,29},{6,30},{7,31},{8,16},{9,... | collective-permute-start | bytes 196616 | tf_op jit(solution)/shard_map/ppermute | solution.py:477
  46.0 0.0 collective-permute-start.20
  46.0 0.8 %collective-permute-start.21 = (f32[2,64,128]{2,1,0:T(8,128)S(1)}, f32[2,64,128]{2,1,0:T(8,128)S(1)}, u32[]{:S(2)}, u32[]{:S(2)}) collective-permute-start(f32[2,64,128]{2,1,0:T(8,128)S(1)} %gradients.1), channel_id=1, source_target_pairs={{0,8},{1,9},{2,10},{3,11},{4,12},{5,13},{6,14},{7,15},{8,0},{9,1},... | collective-permute-start | bytes 196616 | tf_op jit(solution)/shard_map/ppermute | solution.py:477
  46.8 1.9 %collective-permute-done.19 = f32[2,64,128]{2,1,0:T(8,128)S(1)} collective-permute-done((f32[2,64,128]{2,1,0:T(8,128)S(1)}, f32[2,64,128]{2,1,0:T(8,128)S(1)}, u32[]{:S(2)}, u32[]{:S(2)}) %collective-permute-start.19) | collective-permute-done | bytes 65568 | tf_op jit(solution)/shard_map/ppermute | solution.py:477
  48.7 2.4 %collective-permute-done.20 = f32[2,64,128]{2,1,0:T(8,128)S(1)} collective-permute-done((f32[2,64,128]{2,1,0:T(8,128)S(1)}, f32[2,64,128]{2,1,0:T(8,128)S(1)}, u32[]{:S(2)}, u32[]{:S(2)}) %collective-permute-start.20) | collective-permute-done | bytes 65568 | tf_op jit(solution)/shard_map/ppermute | solution.py:477
  51.2 0.0 collective-permute-done.21
  51.2 0.7 %fusion = (f32[1,4,64,128]{3,2,1,0:T(8,128)}, f32[1,4,64,128]{3,2,1,0:T(8,128)}) fusion(f32[2,4,64,128]{3,2,1,0:T(8,128)S(1)} %bitcast_dynamic-update-slice_fusion), kind=kLoop, calls=%fused_computation.4 | loop fusion | bytes 524288 | tf_op jit(solution)/shard_map/slice | solution.py:497
  (12 shorter events, 0.1 us)
Async XLA Ops:
  0.6 8.1 %collective-permute-start = (f32[4,2,32,128]{3,2,1,0:T(8,128)}, f32[4,2,32,128]{3,2,1,0:T(8,128)S(1)}, u32[]{:S(2)}, u32[]{:S(2)}) collective-permute-start(f32[4,2,32,128]{3,2,1,0:T(8,128)} %speed.1), channel_id=1, source_target_pairs={{0,4},{1,5},{2,6},{3,7},{4,0},{5,1},{6,2},{7,3},{8,12},{9,13},{10,... | collective-permute-start | bytes 393224 | tf_op jit(solution)/shard_map/ppermute | solution.py:378
  3.7 6.5 %collective-permute-start.1 = (f32[4,2,32,128]{3,2,1,0:T(8,128)}, f32[4,2,32,128]{3,2,1,0:T(8,128)S(1)}, u32[]{:S(2)}, u32[]{:S(2)}) collective-permute-start(f32[4,2,32,128]{3,2,1,0:T(8,128)} %density.1), channel_id=1, source_target_pairs={{0,4},{1,5},{2,6},{3,7},{4,0},{5,1},{6,2},{7,3},{8,12},{9,13},{10,... | collective-permute-start | bytes 393224 | tf_op jit(solution)/shard_map/ppermute | solution.py:378
  3.7 4.6 %collective-permute-start.2 = (s32[1,4]{1,0:T(1,128)}, s32[1,4]{1,0:T(1,128)S(1)}, u32[]{:S(2)}, u32[]{:S(2)}) collective-permute-start(s32[1,4]{1,0:T(1,128)} %aperture.1), channel_id=1, source_target_pairs={{0,1},{1,0},{2,3},{3,2},{4,5},{5,4},{6,7},{7,6},{8,9},{9,8},{10,11... | collective-permute-start | bytes 56 | tf_op jit(solution)/shard_map/ppermute | solution.py:378
  3.7 4.6 %collective-permute-start.3 = (s32[1,4]{1,0:T(1,128)}, s32[1,4]{1,0:T(1,128)S(1)}, u32[]{:S(2)}, u32[]{:S(2)}) collective-permute-start(s32[1,4]{1,0:T(1,128)} %aperture.1), channel_id=1, source_target_pairs={{0,2},{1,3},{2,0},{3,1},{4,6},{5,7},{6,4},{7,5},{8,10},{9,11},{10,... | collective-permute-start | bytes 56 | tf_op jit(solution)/shard_map/ppermute | solution.py:378
  5.7 3.1 %collective-permute-start.4 = (s32[1,4]{1,0:T(1,128)}, s32[1,4]{1,0:T(1,128)S(1)}, u32[]{:S(2)}, u32[]{:S(2)}) collective-permute-start(s32[1,4]{1,0:T(1,128)} %aperture.1), channel_id=1, source_target_pairs={{0,3},{1,2},{2,1},{3,0},{4,7},{5,6},{6,5},{7,4},{8,11},{9,10},{10,... | collective-permute-start | bytes 56 | tf_op jit(solution)/shard_map/ppermute | solution.py:378
  5.8 0.9 %copy-start.2 = (f32[4,2,32,128]{3,2,1,0:T(8,128)S(1)}, f32[4,2,32,128]{3,2,1,0:T(8,128)}, u32[]{:S(2)}) copy-start(f32[4,2,32,128]{3,2,1,0:T(8,128)} %speed.1) | copy-start | bytes 393220
  6.7 0.9 %copy-start.3 = (f32[4,2,32,128]{3,2,1,0:T(8,128)S(1)}, f32[4,2,32,128]{3,2,1,0:T(8,128)}, u32[]{:S(2)}) copy-start(f32[4,2,32,128]{3,2,1,0:T(8,128)} %density.1) | copy-start | bytes 393220
  7.6 0.7 %copy-start.6 = (s32[1,4]{1,0:T(1,128)S(1)}, s32[1,4]{1,0:T(1,128)}, u32[]{:S(2)}) copy-start(s32[1,4]{1,0:T(1,128)} %aperture.1) | copy-start | bytes 52
  10.2 2.2 %copy-start = (bf16[1,4,8,32,128]{4,3,2,1,0:T(8,128)(2,1)S(1)}, bf16[1,4,8,32,128]{4,3,2,1,0:T(8,128)(2,1)}, u32[]{:S(2)}) copy-start(bf16[1,4,8,32,128]{4,3,2,1,0:T(8,128)(2,1)} %fwd.1) | copy-start | bytes 786436
  10.2 2.2 %copy-start.1 = (bf16[1,4,8,32,128]{4,3,2,1,0:T(8,128)(2,1)S(1)}, bf16[1,4,8,32,128]{4,3,2,1,0:T(8,128)(2,1)}, u32[]{:S(2)}) copy-start(bf16[1,4,8,32,128]{4,3,2,1,0:T(8,128)(2,1)} %adj.1) | copy-start | bytes 786436
  10.2 2.2 %copy-start.8 = (f32[1,4]{1,0:T(1,128)S(1)}, f32[1,4]{1,0:T(1,128)}, u32[]{:S(2)}) copy-start(f32[1,4]{1,0:T(1,128)} %wave.1) | copy-start | bytes 52
  10.4 3.9 %collective-permute-start.5 = (f32[2,2,32,128]{3,2,1,0:T(8,128)S(1)}, f32[2,2,32,128]{3,2,1,0:T(8,128)S(1)}, u32[]{:S(2)}, u32[]{:S(2)}) collective-permute-start(f32[2,2,32,128]{3,2,1,0:T(8,128)S(1)} %get-tuple-element.41), channel_id=1, source_target_pairs={{0,1},{1,0},{2,3},{3,2},{4,5},{5,4},{6,7},{7,6},{8,9},{9,8},{10,11... | collective-permute-start | bytes 196616 | tf_op jit(solution)/shard_map/ppermute | solution.py:378
  10.5 4.5 %collective-permute-start.6 = (f32[2,2,32,128]{3,2,1,0:T(8,128)S(1)}, f32[2,2,32,128]{3,2,1,0:T(8,128)S(1)}, u32[]{:S(2)}, u32[]{:S(2)}) collective-permute-start(f32[2,2,32,128]{3,2,1,0:T(8,128)S(1)} %get-tuple-element.42), channel_id=1, source_target_pairs={{0,2},{1,3},{2,0},{3,1},{4,6},{5,7},{6,4},{7,5},{8,10},{9,11},{10,... | collective-permute-start | bytes 196616 | tf_op jit(solution)/shard_map/ppermute | solution.py:378
  12.3 0.7 %copy-start.4 = (f32[1,4,8]{2,1,0:T(4,128)S(1)}, f32[1,4,8]{2,1,0:T(4,128)}, u32[]{:S(2)}) copy-start(f32[1,4,8]{2,1,0:T(4,128)} %res.1) | copy-start | bytes 388
  12.3 4.0 %collective-permute-start.7 = (f32[2,2,32,128]{3,2,1,0:T(8,128)S(1)}, f32[2,2,32,128]{3,2,1,0:T(8,128)S(1)}, u32[]{:S(2)}, u32[]{:S(2)}) collective-permute-start(f32[2,2,32,128]{3,2,1,0:T(8,128)S(1)} %get-tuple-element.43), channel_id=1, source_target_pairs={{0,3},{1,2},{2,1},{3,0},{4,7},{5,6},{6,5},{7,4},{8,11},{9,10},{10,... | collective-permute-start | bytes 196616 | tf_op jit(solution)/shard_map/ppermute | solution.py:378
  12.3 0.7 %copy-start.5 = (s32[1,8,2]{1,2,0:T(2,128)S(1)}, s32[1,8,2]{1,2,0:T(2,128)}, u32[]{:S(2)}) copy-start(s32[1,8,2]{1,2,0:T(2,128)} %param.16) | copy-start | bytes 196
  12.3 0.7 %copy-start.7 = (s32[1,3]{1,0:T(1,128)S(1)}, s32[1,3]{1,0:T(1,128)}, u32[]{:S(2)}) copy-start(s32[1,3]{1,0:T(1,128)} %src.1) | copy-start | bytes 40
  18.7 1.4 %collective-permute-start.8 = (f32[2,136,128]{2,1,0:T(8,128)S(1)}, f32[2,136,128]{2,1,0:T(8,128)S(1)}, u32[]{:S(2)}, u32[]{:S(2)}) collective-permute-start(f32[2,136,128]{2,1,0:T(8,128)S(1)} %get-tuple-element.59), channel_id=1, source_target_pairs={{0,1},{1,0},{2,3},{3,2},{4,5},{5,4},{6,7},{7,6},{8,9},{9,8},{10,11... | collective-permute-start | bytes 417800 | tf_op jit(solution)/shard_map/ppermute | solution.py:378
  20.1 4.4 %collective-permute-start.10 = (f32[136,128]{1,0:T(8,128)S(1)}, f32[136,128]{1,0:T(8,128)S(1)}, u32[]{:S(2)}, u32[]{:S(2)}) collective-permute-start(f32[136,128]{1,0:T(8,128)S(1)} %get-tuple-element.62), channel_id=1, source_target_pairs={{0,4},{1,5},{2,6},{3,7},{4,0},{5,1},{6,2},{7,3},{8,12},{9,13},{10,... | collective-permute-start | bytes 208904 | tf_op jit(solution)/shard_map/ppermute | solution.py:378
  21.7 5.9 %collective-permute-start.11 = (f32[136,128]{1,0:T(8,128)S(1)}, f32[136,128]{1,0:T(8,128)S(1)}, u32[]{:S(2)}, u32[]{:S(2)}) collective-permute-start(f32[136,128]{1,0:T(8,128)S(1)} %get-tuple-element.63), channel_id=1, source_target_pairs={{0,6},{1,7},{2,4},{3,5},{4,2},{5,3},{6,0},{7,1},{8,14},{9,15},{10,... | collective-permute-start | bytes 208904 | tf_op jit(solution)/shard_map/ppermute | solution.py:378
  23.0 4.6 %collective-permute-start.9 = (f32[136,128]{1,0:T(8,128)S(1)}, f32[136,128]{1,0:T(8,128)S(1)}, u32[]{:S(2)}, u32[]{:S(2)}) collective-permute-start(f32[136,128]{1,0:T(8,128)S(1)} %get-tuple-element.61), channel_id=1, source_target_pairs={{0,2},{1,3},{2,0},{3,1},{4,6},{5,7},{6,4},{7,5},{8,10},{9,11},{10,... | collective-permute-start | bytes 208904 | tf_op jit(solution)/shard_map/ppermute | solution.py:378
  27.8 9.0 %collective-permute-start.12 = (f32[64,128]{1,0:T(8,128)S(1)}, f32[64,128]{1,0:T(8,128)S(1)}, u32[]{:S(2)}, u32[]{:S(2)}) collective-permute-start(f32[64,128]{1,0:T(8,128)S(1)} %get-tuple-element.65), channel_id=1, source_target_pairs={{0,24},{1,25},{2,26},{3,27},{4,28},{5,29},{6,30},{7,31},{8,16},{9,... | collective-permute-start | bytes 98312 | tf_op jit(solution)/shard_map/ppermute | solution.py:477
  31.4 6.9 %collective-permute-start.13 = (f32[64,128]{1,0:T(8,128)S(1)}, f32[64,128]{1,0:T(8,128)S(1)}, u32[]{:S(2)}, u32[]{:S(2)}) collective-permute-start(f32[64,128]{1,0:T(8,128)S(1)} %get-tuple-element.66), channel_id=1, source_target_pairs={{0,28},{1,29},{2,30},{3,31},{4,24},{5,25},{6,26},{7,27},{8,20},{9,... | collective-permute-start | bytes 98312 | tf_op jit(solution)/shard_map/ppermute | solution.py:477
  32.5 7.0 %collective-permute-start.14 = (f32[64,128]{1,0:T(8,128)S(1)}, f32[64,128]{1,0:T(8,128)S(1)}, u32[]{:S(2)}, u32[]{:S(2)}) collective-permute-start(f32[64,128]{1,0:T(8,128)S(1)} %get-tuple-element.67), channel_id=1, source_target_pairs={{0,16},{1,17},{2,18},{3,19},{4,20},{5,21},{6,22},{7,23},{8,24},{9,... | collective-permute-start | bytes 98312 | tf_op jit(solution)/shard_map/ppermute | solution.py:477
  33.3 6.2 %collective-permute-start.15 = (f32[64,128]{1,0:T(8,128)S(1)}, f32[64,128]{1,0:T(8,128)S(1)}, u32[]{:S(2)}, u32[]{:S(2)}) collective-permute-start(f32[64,128]{1,0:T(8,128)S(1)} %get-tuple-element.68), channel_id=1, source_target_pairs={{0,20},{1,21},{2,22},{3,23},{4,16},{5,17},{6,18},{7,19},{8,28},{9,... | collective-permute-start | bytes 98312 | tf_op jit(solution)/shard_map/ppermute | solution.py:477
  35.5 4.0 %collective-permute-start.16 = (f32[64,128]{1,0:T(8,128)S(1)}, f32[64,128]{1,0:T(8,128)S(1)}, u32[]{:S(2)}, u32[]{:S(2)}) collective-permute-start(f32[64,128]{1,0:T(8,128)S(1)} %get-tuple-element.69), channel_id=1, source_target_pairs={{0,8},{1,9},{2,10},{3,11},{4,12},{5,13},{6,14},{7,15},{8,0},{9,1},... | collective-permute-start | bytes 98312 | tf_op jit(solution)/shard_map/ppermute | solution.py:477
  36.7 4.8 %collective-permute-start.17 = (f32[64,128]{1,0:T(8,128)S(1)}, f32[64,128]{1,0:T(8,128)S(1)}, u32[]{:S(2)}, u32[]{:S(2)}) collective-permute-start(f32[64,128]{1,0:T(8,128)S(1)} %get-tuple-element.70), channel_id=1, source_target_pairs={{0,12},{1,13},{2,14},{3,15},{4,8},{5,9},{6,10},{7,11},{8,4},{9,5},... | collective-permute-start | bytes 98312 | tf_op jit(solution)/shard_map/ppermute | solution.py:477
  38.3 3.9 %collective-permute-start.18 = (f32[64,128]{1,0:T(8,128)S(1)}, f32[64,128]{1,0:T(8,128)S(1)}, u32[]{:S(2)}, u32[]{:S(2)}) collective-permute-start(f32[64,128]{1,0:T(8,128)S(1)} %get-tuple-element.71), channel_id=1, source_target_pairs={{0,4},{1,5},{2,6},{3,7},{4,0},{5,1},{6,2},{7,3},{8,12},{9,13},{10,... | collective-permute-start | bytes 98312 | tf_op jit(solution)/shard_map/ppermute | solution.py:477
  42.3 6.4 %collective-permute-start.19 = (f32[2,64,128]{2,1,0:T(8,128)S(1)}, f32[2,64,128]{2,1,0:T(8,128)S(1)}, u32[]{:S(2)}, u32[]{:S(2)}) collective-permute-start(f32[2,64,128]{2,1,0:T(8,128)S(1)} %gradients.1), channel_id=1, source_target_pairs={{0,24},{1,25},{2,26},{3,27},{4,28},{5,29},{6,30},{7,31},{8,16},{9,... | collective-permute-start | bytes 196616 | tf_op jit(solution)/shard_map/ppermute | solution.py:477
  46.0 5.2 %collective-permute-start.20 = (f32[2,64,128]{2,1,0:T(8,128)S(1)}, f32[2,64,128]{2,1,0:T(8,128)S(1)}, u32[]{:S(2)}, u32[]{:S(2)}) collective-permute-start(f32[2,64,128]{2,1,0:T(8,128)S(1)} %gradients.1), channel_id=1, source_target_pairs={{0,16},{1,17},{2,18},{3,19},{4,20},{5,21},{6,22},{7,23},{8,24},{9,... | collective-permute-start | bytes 196616 | tf_op jit(solution)/shard_map/ppermute | solution.py:477
  46.0 5.2 %collective-permute-start.21 = (f32[2,64,128]{2,1,0:T(8,128)S(1)}, f32[2,64,128]{2,1,0:T(8,128)S(1)}, u32[]{:S(2)}, u32[]{:S(2)}) collective-permute-start(f32[2,64,128]{2,1,0:T(8,128)S(1)} %gradients.1), channel_id=1, source_target_pairs={{0,8},{1,9},{2,10},{3,11},{4,12},{5,13},{6,14},{7,15},{8,0},{9,1},... | collective-permute-start | bytes 196616 | tf_op jit(solution)/shard_map/ppermute | solution.py:477
where the time goes:
time: 52.1 us; the launch traced here: 51.9 us
  starting transfers between devices  27 us (52%)
  waiting for transfers between devices  16 us (31%)
  Pallas kernels  4.13 us (8%)
  local copies, waits for them, and re-layouts  3.93 us (8%)
  between operations  0.78 us (1%)
    ppermute x10, starting transfers between devices, along(): return lax.ppermute(values, ('grp', 'tile'), pairs)  16.1 us
    ppermute x12, starting transfers between devices, across(): return lax.ppermute(values, 'tile', [(t, t ^ hop) for t in range(owners)])  10.9 us
    ppermute x12, waiting for transfers between devices, across(): return lax.ppermute(values, 'tile', [(t, t ^ hop) for t in range(owners)])  8.9 us
    ppermute x10, waiting for transfers between devices, along(): return lax.ppermute(values, ('grp', 'tile'), pairs)  7.14 us
    unnamed x18, local copies, waits for them, and re-layouts  3.14 us
    pallas_call x1, Pallas kernels, per_device(): pl.pallas_call(functools.partial(wave_kernel, chips, steps, held), out_sh...  2.34 us
    pallas_call x1, Pallas kernels, per_device(): pl.pallas_call(functools.partial(prepare_kernel, steps), out_shape=[shape...  1.28 us
  transfers between devices with their start and end apart: 22, of which 11 were waited for; matrix products, arithmetic and copies ran while one was open for 0% of the time, Pallas kernels for 3%

commit v1 on v0

--- a/solution.py
+++ b/solution.py
@@ -317,9 +317,9 @@
 def add_kernel(stripes, groups, held, *refs):
     came, parts, total = refs[:stripes], refs[stripes:-1], refs[-1]
     me, group = lax.axis_index("tile"), lax.axis_index("grp")
-    residue, half = lax.rem(me, stripes), lax.div(me, stripes)
+    residue = lax.rem(me, stripes)
     tile_rows = total.shape[0] // (2 * held)
-    part = parts[0].shape[0]
+    part = parts[0].shape[1]
     total[...] = jnp.zeros_like(total)
     for pair in came:
         for shot in range(2):
@@ -329,32 +329,33 @@
             slot = jnp.where(residue < corner, held, 0) + column
             rows = pl.ds(pl.multiple_of(slot * tile_rows, tile_rows), tile_rows)
             total[rows] = total[rows] + pair[shot * tile_rows : (shot + 1) * tile_rows]
-    for out, (hop, flip) in zip(parts, part_order(groups)):
-        owner = jnp.where(half == flip, 0, 1)
-        first = owner * (held * tile_rows) + (group ^ hop) * part
-        out[...] = total[pl.ds(pl.multiple_of(first, part), part)]
-
-
-def part_order(groups):
-    hops = [(hop, flip) for hop in far_first(groups) for flip in range(2)]
-    return [(0, 0)] + hops + [(0, 1)]
+    for out, hop in zip(parts, [0] + far_first(groups)):
+        for owner in range(2):
+            first = owner * (held * tile_rows) + (group ^ hop) * part
+            out[owner] = total[pl.ds(pl.multiple_of(first, part), part)]
 
 
 def far_first(groups):
     return list(range(groups - 1, 0, -1))
 
 
-def grads_kernel(scale, groups, stripes, *refs):
-    parts, speed_ref, density_ref, grads = refs[: 2 * groups], *refs[2 * groups :]
-    part = parts[0].shape[0]
+def sum_kernel(stripes, *refs):
+    parts, (mine, other) = refs[:-2], refs[-2:]
+    sums = parts[0][...]
+    for values in parts[1:]:
+        sums = sums + values[...]
+    first_half = lax.axis_index("tile") < stripes
+    mine[...] = jnp.where(first_half, sums[0], sums[1])
+    other[...] = jnp.where(first_half, sums[1], sums[0])
+
+
+def grads_kernel(scale, stripes, mine, came, speed_ref, density_ref, grads):
+    part = mine.shape[0]
     rows = pl.ds(pl.multiple_of(lax.axis_index("grp") * part, part), part)
     speed, density = speed_ref[rows], density_ref[rows]
-    sums = [None, None]
-    for values, (_, flip) in zip(parts, part_order(groups)):
-        sums[flip] = values[...] if sums[flip] is None else sums[flip] + values[...]
     first_half = lax.axis_index("tile") < stripes
-    bulk_sum = jnp.where(first_half, sums[0], sums[1])
-    buoy_sum = jnp.where(first_half, sums[1], sums[0])
+    bulk_sum = jnp.where(first_half, mine[...], came[...])
+    buoy_sum = jnp.where(first_half, came[...], mine[...])
     grads[0] = scale * (bulk_sum * (2.0 * density * speed))
     grads[1] = scale * (bulk_sum * (speed * speed) - buoy_sum / (density * density))
 
@@ -454,40 +455,46 @@
         compiler_params=PARAMS,
         name="merge_pair",
     )(kept, across(traded, 1))
-    came = [across(stacks[chip], 2 * chip) if chip else stacks[0] for chip in range(stripes)]
+    order = [1] + list(range(stripes - 1, 1, -1))
+    came = [stacks[0]] + [across(stacks[chip], 2 * chip) for chip in order]
 
     rows = held * tile_rows
     part = rows // groups
     parts = pl.pallas_call(
         functools.partial(add_kernel, stripes, groups, held),
-        out_shape=[shape(part, depth)] * (2 * groups),
+        out_shape=[shape(2, part, depth)] * groups,
         in_specs=[VMEM] * stripes,
-        out_specs=[VMEM] * (2 * groups),
+        out_specs=[VMEM] * groups,
         scratch_shapes=[pltpu.VMEM((2 * rows, depth), f32)],
         compiler_params=PARAMS,
         name="add_stripes",
     )(*came)
 
-    def along(values, hop, flip=0):
-        pairs = [
-            (g * owners + t, (g ^ hop) * owners + (t ^ (flip * stripes)))
-            for g in range(groups)
-            for t in range(owners)
-        ]
-        return lax.ppermute(values, ("grp", "tile"), pairs)
-
-    parts = [
-        along(values, *hops) if any(hops) else values
-        for values, hops in zip(parts, part_order(groups))
-    ]
+    def along(values, hop):
+        return lax.ppermute(values, "grp", [(g, g ^ hop) for g in range(groups)])
+
+    parts = [parts[0]] + [along(values, hop) for values, hop in zip(parts[1:], far_first(groups))]
+    mine, other = pl.pallas_call(
+        functools.partial(sum_kernel, stripes),
+        out_shape=[shape(part, depth)] * 2,
+        in_specs=[VMEM] * groups,
+        out_specs=[VMEM] * 2,
+        compiler_params=PARAMS,
+        name="sum_groups",
+    )(*parts)
     grads = pl.pallas_call(
-        functools.partial(grads_kernel, 1.0 / math.sqrt(groups * owners), groups, stripes),
+        functools.partial(grads_kernel, 1.0 / math.sqrt(groups * owners), stripes),
         out_shape=shape(2, part, depth),
-        in_specs=[VMEM] * (2 * groups + 2),
+        in_specs=[VMEM] * 4,
         out_specs=VMEM,
         compiler_params=PARAMS,
         name="gradients",
-    )(*parts, near_speed.reshape(rows, depth), near_density.reshape(rows, depth))
+    )(
+        mine,
+        across(other, stripes),
+        near_speed.reshape(rows, depth),
+        near_density.reshape(rows, depth),
+    )
 
     whole = jnp.zeros((2, groups, part, depth), f32)
     for hop in [0] + far_first(groups):

time: 52.1 us -> 49.3 us (0.946)
  starting transfers between devices: 27 us -> 21.5 us
  waiting for transfers between devices: 16 us -> 18.8 us
    ppermute x10 -> x6, starting transfers between devices: 16.1 us -> 8.91 us  [along(): return lax.ppermute(values, 'grp', [(g, g ^ hop) for g in range(groups)])]
    ppermute x12 -> x13, waiting for transfers between devices: 8.9 us -> 11 us  [across(): return lax.ppermute(values, 'tile', [(t, t ^ hop) for t in range(owners)])]
    ppermute x12 -> x13, starting transfers between devices: 10.9 us -> 12.5 us  [across(): return lax.ppermute(values, 'tile', [(t, t ^ hop) for t in range(owners)])]
    ppermute x10 -> x6, waiting for transfers between devices: 7.14 us -> 7.83 us  [along(): return lax.ppermute(values, 'grp', [(g, g ^ hop) for g in range(groups)])]
  transfers between devices with their start and end apart: 22 -> 19, of which waited for: 11 -> 13; matrix products, arithmetic and copies ran while one was open for 0% -> 0% of each run, Pallas kernels for 3% -> 3%
where the time goes in v1:
time: 49.3 us; the launch traced here: 49.1 us
  starting transfers between devices  21.5 us (44%)
  waiting for transfers between devices  18.8 us (38%)
  Pallas kernels  4.14 us (8%)
  local copies, waits for them, and re-layouts  3.93 us (8%)
  between operations  0.78 us (2%)
    ppermute x13, starting transfers between devices, across(): return lax.ppermute(values, 'tile', [(t, t ^ hop) for t in range(owners)])  12.5 us
    ppermute x13, waiting for transfers between devices, across(): return lax.ppermute(values, 'tile', [(t, t ^ hop) for t in range(owners)])  11 us
    ppermute x6, starting transfers between devices, along(): return lax.ppermute(values, 'grp', [(g, g ^ hop) for g in range(groups)])  8.91 us
    ppermute x6, waiting for transfers between devices, along(): return lax.ppermute(values, 'grp', [(g, g ^ hop) for g in range(groups)])  7.83 us
    unnamed x18, local copies, waits for them, and re-layouts  3.14 us
    pallas_call x1, Pallas kernels, per_device(): pl.pallas_call(functools.partial(wave_kernel, chips, steps, held), out_sh...  2.35 us
    pallas_call x1, Pallas kernels, per_device(): pl.pallas_call(functools.partial(prepare_kernel, steps), out_shape=[shape...  1.28 us
  transfers between devices with their start and end apart: 19, of which 13 were waited for; matrix products, arithmetic and copies ran while one was open for 0% of the time, Pallas kernels for 3%

profile of v1, /device:TPU:0, one launch (start us, length us, event | category | flops | bytes accessed | tf_op | source)
XLA Modules:
  0.0 49.1 jit_solution(11700682420561690211)
XLA Ops:
  0.6 3.0 %collective-permute-start = (f32[4,2,32,128]{3,2,1,0:T(8,128)}, f32[4,2,32,128]{3,2,1,0:T(8,128)S(1)}, u32[]{:S(2)}, u32[]{:S(2)}) collective-permute-start(f32[4,2,32,128]{3,2,1,0:T(8,128)} %speed.1), channel_id=1, source_target_pairs={{0,4},{1,5},{2,6},{3,7},{4,0},{5,1},{6,2},{7,3},{8,12},{9,13},{10,... | collective-permute-start | bytes 393224 | tf_op jit(solution)/shard_map/ppermute | solution.py:379
  3.7 0.1 collective-permute-start.1
  3.7 0.0 collective-permute-start.2
  3.7 1.9 %collective-permute-start.3 = (s32[1,4]{1,0:T(1,128)}, s32[1,4]{1,0:T(1,128)S(1)}, u32[]{:S(2)}, u32[]{:S(2)}) collective-permute-start(s32[1,4]{1,0:T(1,128)} %aperture.1), channel_id=1, source_target_pairs={{0,2},{1,3},{2,0},{3,1},{4,6},{5,7},{6,4},{7,5},{8,10},{9,11},{10,... | collective-permute-start | bytes 56 | tf_op jit(solution)/shard_map/ppermute | solution.py:379
  5.7 0.2 collective-permute-start.4
  5.8 0.0 copy-start.2
  5.8 0.9 %copy-done.2 = f32[4,2,32,128]{3,2,1,0:T(8,128)S(1)} copy-done((f32[4,2,32,128]{3,2,1,0:T(8,128)S(1)}, f32[4,2,32,128]{3,2,1,0:T(8,128)}, u32[]{:S(2)}) %copy-start.2) | copy-done | bytes 131096
  6.7 0.0 copy-start.3
  6.7 0.9 %copy-done.3 = f32[4,2,32,128]{3,2,1,0:T(8,128)S(1)} copy-done((f32[4,2,32,128]{3,2,1,0:T(8,128)S(1)}, f32[4,2,32,128]{3,2,1,0:T(8,128)}, u32[]{:S(2)}) %copy-start.3) | copy-done | bytes 131096
  7.6 0.0 copy-start.6
  7.6 0.7 %copy-done.6 = s32[1,4]{1,0:T(1,128)S(1)} copy-done((s32[1,4]{1,0:T(1,128)S(1)}, s32[1,4]{1,0:T(1,128)}, u32[]{:S(2)}) %copy-start.6) | copy-done | bytes 40
  8.3 0.1 hold_near_tiles.1
  8.4 0.0 collective-permute-done.2.refs_1_
  8.4 0.0 collective-permute-done.3.refs_2_
  8.4 0.4 collective-permute-done.4.refs_3_
  8.8 0.0 collective-permute-done.far_speed
  8.8 1.4 %collective-permute-done.1.far_density = f32[4,2,32,128]{3,2,1,0:T(8,128)S(1)} collective-permute-done((f32[4,2,32,128]{3,2,1,0:T(8,128)}, f32[4,2,32,128]{3,2,1,0:T(8,128)S(1)}, u32[]{:S(2)}, u32[]{:S(2)}) %collective-permute-start.1) | collective-permute-done | bytes 131104 | tf_op jit(solution)/shard_map/ppermute | solution.py:379
  10.2 0.0 copy-start
  10.2 0.0 copy-start.1
  10.2 0.0 copy-start.8
  10.2 0.2 pick_tiles.1
  10.4 0.1 collective-permute-start.5
  10.5 1.8 %collective-permute-start.6 = (f32[2,2,32,128]{3,2,1,0:T(8,128)S(1)}, f32[2,2,32,128]{3,2,1,0:T(8,128)S(1)}, u32[]{:S(2)}, u32[]{:S(2)}) collective-permute-start(f32[2,2,32,128]{3,2,1,0:T(8,128)S(1)} %get-tuple-element.40), channel_id=1, source_target_pairs={{0,2},{1,3},{2,0},{3,1},{4,6},{5,7},{6,4},{7,5},{8,10},{9,11},{10,... | collective-permute-start | bytes 196616 | tf_op jit(solution)/shard_map/ppermute | solution.py:379
  12.3 0.0 copy-start.4
  12.3 0.1 collective-permute-start.7
  12.3 0.0 copy-start.5
  12.3 0.0 copy-start.7
  12.3 0.0 copy-done
  12.4 0.0 copy-done.1
  12.4 0.0 copy-done.8
  12.4 0.6 %copy-done.4 = f32[1,4,8]{2,1,0:T(4,128)S(1)} copy-done((f32[1,4,8]{2,1,0:T(4,128)S(1)}, f32[1,4,8]{2,1,0:T(4,128)}, u32[]{:S(2)}) %copy-start.4) | copy-done | bytes 152
  12.9 0.1 copy-done.5
  13.0 0.0 copy-done.7
  13.0 1.3 %prepare.1 = (f32[3,8,32,128]{3,2,1,0:T(8,128)S(1)}, f32[3,8,32,128]{3,2,1,0:T(8,128)S(1)}, f32[4,8,32,128]{3,2,1,0:T(8,128)S(1)}, f32[4,8,32,128]{3,2,1,0:T(8,1...) custom-call(bf16[1,4,8,32,128]{4,3,2,1,0:T(8,128)(2,1)S(1)} %copy-do, ...), custom_call_target="tpu_custom_call" | custom-call | flops 4000000 | bytes 6000000 | tf_op jit(solution)/shard_map/prepare/pallas_call | solution.py:413
  14.3 0.0 collective-permute-done.5.refs_1_
  14.3 0.7 %collective-permute-done.6.refs_2_ = f32[2,2,32,128]{3,2,1,0:T(8,128)S(1)} collective-permute-done((f32[2,2,32,128]{3,2,1,0:T(8,128)S(1)}, f32[2,2,32,128]{3,2,1,0:T(8,128)S(1)}, u32[]{:S(2)}, u32[]{:S(2)}) %collective-permute-start.6) | collective-permute-done | bytes 65568 | tf_op jit(solution)/shard_map/ppermute | solution.py:379
  15.0 1.3 %collective-permute-done.7.refs_3_ = f32[2,2,32,128]{3,2,1,0:T(8,128)S(1)} collective-permute-done((f32[2,2,32,128]{3,2,1,0:T(8,128)S(1)}, f32[2,2,32,128]{3,2,1,0:T(8,128)S(1)}, u32[]{:S(2)}, u32[]{:S(2)}) %collective-permute-start.7) | collective-permute-done | bytes 65568 | tf_op jit(solution)/shard_map/ppermute | solution.py:379
  16.3 2.3 %replay_and_adjoint.1 = (f32[2,136,128]{2,1,0:T(8,128)S(1)}, f32[2,136,128]{2,1,0:T(8,128)S(1)}, f32[16,48,128]{2,1,0:T(8,128)S(1)}, f32[16,32,128]{2,1,0:T(8,12...) custom-call(f32[2,2,32,128]{3,2,1,0:T(8,128)S(1)} %get-tuple-element, ...), custom_call_target="tpu_custom_call", output_to_operand_aliasing={{2}: (11, {}), {3}: (12, {}), {4}: (13, {}), {5}: (14, {}),... | custom-call | tf_op jit(solution)/shard_map/replay_and_adjoint/pallas_call | solution.py:430
  18.7 0.2 collective-permute-start.8
  18.9 1.2 %collective-permute-done.8.came = f32[2,136,128]{2,1,0:T(8,128)S(1)} collective-permute-done((f32[2,136,128]{2,1,0:T(8,128)S(1)}, f32[2,136,128]{2,1,0:T(8,128)S(1)}, u32[]{:S(2)}, u32[]{:S(2)}) %collective-permute-start.8) | collective-permute-done | bytes 139296 | tf_op jit(solution)/shard_map/ppermute | solution.py:379
  20.1 2.4 %collective-permute-start.10 = (f32[136,128]{1,0:T(8,128)S(1)}, f32[136,128]{1,0:T(8,128)S(1)}, u32[]{:S(2)}, u32[]{:S(2)}) collective-permute-start(f32[136,128]{1,0:T(8,128)S(1)} %get-tuple-element.60), channel_id=1, source_target_pairs={{0,6},{1,7},{2,4},{3,5},{4,2},{5,3},{6,0},{7,1},{8,14},{9,15},{10,... | collective-permute-start | bytes 208904 | tf_op jit(solution)/shard_map/ppermute | solution.py:379
  22.5 0.5 %collective-permute-start.11 = (f32[136,128]{1,0:T(8,128)S(1)}, f32[136,128]{1,0:T(8,128)S(1)}, u32[]{:S(2)}, u32[]{:S(2)}) collective-permute-start(f32[136,128]{1,0:T(8,128)S(1)} %get-tuple-element.61), channel_id=1, source_target_pairs={{0,4},{1,5},{2,6},{3,7},{4,0},{5,1},{6,2},{7,3},{8,12},{9,13},{10,... | collective-permute-start | bytes 208904 | tf_op jit(solution)/shard_map/ppermute | solution.py:379
  23.0 0.7 %collective-permute-start.9 = (f32[136,128]{1,0:T(8,128)S(1)}, f32[136,128]{1,0:T(8,128)S(1)}, u32[]{:S(2)}, u32[]{:S(2)}) collective-permute-start(f32[136,128]{1,0:T(8,128)S(1)} %get-tuple-element.59), channel_id=1, source_target_pairs={{0,2},{1,3},{2,0},{3,1},{4,6},{5,7},{6,4},{7,5},{8,10},{9,11},{10,... | collective-permute-start | bytes 208904 | tf_op jit(solution)/shard_map/ppermute | solution.py:379
  23.7 1.8 %collective-permute-done.10.refs_2_ = f32[136,128]{1,0:T(8,128)S(1)} collective-permute-done((f32[136,128]{1,0:T(8,128)S(1)}, f32[136,128]{1,0:T(8,128)S(1)}, u32[]{:S(2)}, u32[]{:S(2)}) %collective-permute-start.10) | collective-permute-done | bytes 69664 | tf_op jit(solution)/shard_map/ppermute | solution.py:379
  25.4 1.5 %collective-permute-done.11.refs_3_ = f32[136,128]{1,0:T(8,128)S(1)} collective-permute-done((f32[136,128]{1,0:T(8,128)S(1)}, f32[136,128]{1,0:T(8,128)S(1)}, u32[]{:S(2)}, u32[]{:S(2)}) %collective-permute-start.11) | collective-permute-done | bytes 69664 | tf_op jit(solution)/shard_map/ppermute | solution.py:379
  26.9 0.4 collective-permute-done.9.refs_1_
  27.3 0.2 add_stripes.1
  27.5 3.7 %collective-permute-start.12 = (f32[2,64,128]{2,1,0:T(8,128)S(1)}, f32[2,64,128]{2,1,0:T(8,128)S(1)}, u32[]{:S(2)}, u32[]{:S(2)}) collective-permute-start(f32[2,64,128]{2,1,0:T(8,128)S(1)} %get-tuple-element.63), channel_id=1, source_target_pairs={{0,24},{8,16},{16,8},{24,0},{1,25},{9,17},{17,9},{25,1},{2,26},{10... | collective-permute-start | bytes 196616 | tf_op jit(solution)/shard_map/ppermute | solution.py:474
  31.2 0.0 collective-permute-start.13
  31.2 0.8 %collective-permute-start.14 = (f32[2,64,128]{2,1,0:T(8,128)S(1)}, f32[2,64,128]{2,1,0:T(8,128)S(1)}, u32[]{:S(2)}, u32[]{:S(2)}) collective-permute-start(f32[2,64,128]{2,1,0:T(8,128)S(1)} %get-tuple-element.65), channel_id=1, source_target_pairs={{0,8},{8,0},{16,24},{24,16},{1,9},{9,1},{17,25},{25,17},{2,10},{10... | collective-permute-start | bytes 196616 | tf_op jit(solution)/shard_map/ppermute | solution.py:474
  31.9 2.0 %collective-permute-done.12.refs_1_ = f32[2,64,128]{2,1,0:T(8,128)S(1)} collective-permute-done((f32[2,64,128]{2,1,0:T(8,128)S(1)}, f32[2,64,128]{2,1,0:T(8,128)S(1)}, u32[]{:S(2)}, u32[]{:S(2)}) %collective-permute-start.12) | collective-permute-done | bytes 65568 | tf_op jit(solution)/shard_map/ppermute | solution.py:474
  33.9 2.6 %collective-permute-done.13.refs_2_ = f32[2,64,128]{2,1,0:T(8,128)S(1)} collective-permute-done((f32[2,64,128]{2,1,0:T(8,128)S(1)}, f32[2,64,128]{2,1,0:T(8,128)S(1)}, u32[]{:S(2)}, u32[]{:S(2)}) %collective-permute-start.13) | collective-permute-done | bytes 65568 | tf_op jit(solution)/shard_map/ppermute | solution.py:474
  36.5 0.0 collective-permute-done.14.refs_3_
  36.5 1.6 %collective-permute-start.15 = (f32[64,128]{1,0:T(8,128)S(1)}, f32[64,128]{1,0:T(8,128)S(1)}, u32[]{:S(2)}, u32[]{:S(2)}) collective-permute-start(f32[64,128]{1,0:T(8,128)S(1)} %get-tuple-element.67), channel_id=1, source_target_pairs={{0,4},{1,5},{2,6},{3,7},{4,0},{5,1},{6,2},{7,3},{8,12},{9,13},{10,... | collective-permute-start | bytes 98312 | tf_op jit(solution)/shard_map/ppermute | solution.py:379
  38.2 2.3 %collective-permute-done.15.came = f32[64,128]{1,0:T(8,128)S(1)} collective-permute-done((f32[64,128]{1,0:T(8,128)S(1)}, f32[64,128]{1,0:T(8,128)S(1)}, u32[]{:S(2)}, u32[]{:S(2)}) %collective-permute-start.15) | collective-permute-done | bytes 32800 | tf_op jit(solution)/shard_map/ppermute | solution.py:379
  40.5 2.4 %collective-permute-start.16 = (f32[2,64,128]{2,1,0:T(8,128)S(1)}, f32[2,64,128]{2,1,0:T(8,128)S(1)}, u32[]{:S(2)}, u32[]{:S(2)}) collective-permute-start(f32[2,64,128]{2,1,0:T(8,128)S(1)} %gradients.1), channel_id=1, source_target_pairs={{0,24},{8,16},{16,8},{24,0},{1,25},{9,17},{17,9},{25,1},{2,26},{10... | collective-permute-start | bytes 196616 | tf_op jit(solution)/shard_map/ppermute | solution.py:474
  42.9 0.0 collective-permute-start.17
  42.9 2.1 %collective-permute-start.18 = (f32[2,64,128]{2,1,0:T(8,128)S(1)}, f32[2,64,128]{2,1,0:T(8,128)S(1)}, u32[]{:S(2)}, u32[]{:S(2)}) collective-permute-start(f32[2,64,128]{2,1,0:T(8,128)S(1)} %gradients.1), channel_id=1, source_target_pairs={{0,8},{8,0},{16,24},{24,16},{1,9},{9,1},{17,25},{25,17},{2,10},{10... | collective-permute-start | bytes 196616 | tf_op jit(solution)/shard_map/ppermute | solution.py:474
  45.0 1.6 %collective-permute-done.16 = f32[2,64,128]{2,1,0:T(8,128)S(1)} collective-permute-done((f32[2,64,128]{2,1,0:T(8,128)S(1)}, f32[2,64,128]{2,1,0:T(8,128)S(1)}, u32[]{:S(2)}, u32[]{:S(2)}) %collective-permute-start.16) | collective-permute-done | bytes 65568 | tf_op jit(solution)/shard_map/ppermute | solution.py:474
  46.7 1.6 %collective-permute-done.17 = f32[2,64,128]{2,1,0:T(8,128)S(1)} collective-permute-done((f32[2,64,128]{2,1,0:T(8,128)S(1)}, f32[2,64,128]{2,1,0:T(8,128)S(1)}, u32[]{:S(2)}, u32[]{:S(2)}) %collective-permute-start.17) | collective-permute-done | bytes 65568 | tf_op jit(solution)/shard_map/ppermute | solution.py:474
  48.3 0.0 collective-permute-done.18
  48.4 0.7 %fusion = (f32[1,4,64,128]{3,2,1,0:T(8,128)}, f32[1,4,64,128]{3,2,1,0:T(8,128)}) fusion(f32[2,4,64,128]{3,2,1,0:T(8,128)S(1)} %bitcast_dynamic-update-slice_fusion), kind=kLoop, calls=%fused_computation.4 | loop fusion | bytes 524288 | tf_op jit(solution)/shard_map/slice | solution.py:504
  (9 shorter events, 0.1 us)
Async XLA Ops:
  0.6 8.1 %collective-permute-start = (f32[4,2,32,128]{3,2,1,0:T(8,128)}, f32[4,2,32,128]{3,2,1,0:T(8,128)S(1)}, u32[]{:S(2)}, u32[]{:S(2)}) collective-permute-start(f32[4,2,32,128]{3,2,1,0:T(8,128)} %speed.1), channel_id=1, source_target_pairs={{0,4},{1,5},{2,6},{3,7},{4,0},{5,1},{6,2},{7,3},{8,12},{9,13},{10,... | collective-permute-start | bytes 393224 | tf_op jit(solution)/shard_map/ppermute | solution.py:379
  3.7 6.5 %collective-permute-start.1 = (f32[4,2,32,128]{3,2,1,0:T(8,128)}, f32[4,2,32,128]{3,2,1,0:T(8,128)S(1)}, u32[]{:S(2)}, u32[]{:S(2)}) collective-permute-start(f32[4,2,32,128]{3,2,1,0:T(8,128)} %density.1), channel_id=1, source_target_pairs={{0,4},{1,5},{2,6},{3,7},{4,0},{5,1},{6,2},{7,3},{8,12},{9,13},{10,... | collective-permute-start | bytes 393224 | tf_op jit(solution)/shard_map/ppermute | solution.py:379
  3.7 4.6 %collective-permute-start.2 = (s32[1,4]{1,0:T(1,128)}, s32[1,4]{1,0:T(1,128)S(1)}, u32[]{:S(2)}, u32[]{:S(2)}) collective-permute-start(s32[1,4]{1,0:T(1,128)} %aperture.1), channel_id=1, source_target_pairs={{0,1},{1,0},{2,3},{3,2},{4,5},{5,4},{6,7},{7,6},{8,9},{9,8},{10,11... | collective-permute-start | bytes 56 | tf_op jit(solution)/shard_map/ppermute | solution.py:379
  3.7 4.6 %collective-permute-start.3 = (s32[1,4]{1,0:T(1,128)}, s32[1,4]{1,0:T(1,128)S(1)}, u32[]{:S(2)}, u32[]{:S(2)}) collective-permute-start(s32[1,4]{1,0:T(1,128)} %aperture.1), channel_id=1, source_target_pairs={{0,2},{1,3},{2,0},{3,1},{4,6},{5,7},{6,4},{7,5},{8,10},{9,11},{10,... | collective-permute-start | bytes 56 | tf_op jit(solution)/shard_map/ppermute | solution.py:379
  5.7 3.1 %collective-permute-start.4 = (s32[1,4]{1,0:T(1,128)}, s32[1,4]{1,0:T(1,128)S(1)}, u32[]{:S(2)}, u32[]{:S(2)}) collective-permute-start(s32[1,4]{1,0:T(1,128)} %aperture.1), channel_id=1, source_target_pairs={{0,3},{1,2},{2,1},{3,0},{4,7},{5,6},{6,5},{7,4},{8,11},{9,10},{10,... | collective-permute-start | bytes 56 | tf_op jit(solution)/shard_map/ppermute | solution.py:379
  5.8 0.9 %copy-start.2 = (f32[4,2,32,128]{3,2,1,0:T(8,128)S(1)}, f32[4,2,32,128]{3,2,1,0:T(8,128)}, u32[]{:S(2)}) copy-start(f32[4,2,32,128]{3,2,1,0:T(8,128)} %speed.1) | copy-start | bytes 393220
  6.7 0.9 %copy-start.3 = (f32[4,2,32,128]{3,2,1,0:T(8,128)S(1)}, f32[4,2,32,128]{3,2,1,0:T(8,128)}, u32[]{:S(2)}) copy-start(f32[4,2,32,128]{3,2,1,0:T(8,128)} %density.1) | copy-start | bytes 393220
  7.6 0.7 %copy-start.6 = (s32[1,4]{1,0:T(1,128)S(1)}, s32[1,4]{1,0:T(1,128)}, u32[]{:S(2)}) copy-start(s32[1,4]{1,0:T(1,128)} %aperture.1) | copy-start | bytes 52
  10.2 2.2 %copy-start = (bf16[1,4,8,32,128]{4,3,2,1,0:T(8,128)(2,1)S(1)}, bf16[1,4,8,32,128]{4,3,2,1,0:T(8,128)(2,1)}, u32[]{:S(2)}) copy-start(bf16[1,4,8,32,128]{4,3,2,1,0:T(8,128)(2,1)} %fwd.1) | copy-start | bytes 786436
  10.2 2.2 %copy-start.1 = (bf16[1,4,8,32,128]{4,3,2,1,0:T(8,128)(2,1)S(1)}, bf16[1,4,8,32,128]{4,3,2,1,0:T(8,128)(2,1)}, u32[]{:S(2)}) copy-start(bf16[1,4,8,32,128]{4,3,2,1,0:T(8,128)(2,1)} %adj.1) | copy-start | bytes 786436
  10.2 2.2 %copy-start.8 = (f32[1,4]{1,0:T(1,128)S(1)}, f32[1,4]{1,0:T(1,128)}, u32[]{:S(2)}) copy-start(f32[1,4]{1,0:T(1,128)} %wave.1) | copy-start | bytes 52
  10.4 3.9 %collective-permute-start.5 = (f32[2,2,32,128]{3,2,1,0:T(8,128)S(1)}, f32[2,2,32,128]{3,2,1,0:T(8,128)S(1)}, u32[]{:S(2)}, u32[]{:S(2)}) collective-permute-start(f32[2,2,32,128]{3,2,1,0:T(8,128)S(1)} %get-tuple-element.39), channel_id=1, source_target_pairs={{0,1},{1,0},{2,3},{3,2},{4,5},{5,4},{6,7},{7,6},{8,9},{9,8},{10,11... | collective-permute-start | bytes 196616 | tf_op jit(solution)/shard_map/ppermute | solution.py:379
  10.5 4.5 %collective-permute-start.6 = (f32[2,2,32,128]{3,2,1,0:T(8,128)S(1)}, f32[2,2,32,128]{3,2,1,0:T(8,128)S(1)}, u32[]{:S(2)}, u32[]{:S(2)}) collective-permute-start(f32[2,2,32,128]{3,2,1,0:T(8,128)S(1)} %get-tuple-element.40), channel_id=1, source_target_pairs={{0,2},{1,3},{2,0},{3,1},{4,6},{5,7},{6,4},{7,5},{8,10},{9,11},{10,... | collective-permute-start | bytes 196616 | tf_op jit(solution)/shard_map/ppermute | solution.py:379
  12.3 0.7 %copy-start.4 = (f32[1,4,8]{2,1,0:T(4,128)S(1)}, f32[1,4,8]{2,1,0:T(4,128)}, u32[]{:S(2)}) copy-start(f32[1,4,8]{2,1,0:T(4,128)} %res.1) | copy-start | bytes 388
  12.3 4.0 %collective-permute-start.7 = (f32[2,2,32,128]{3,2,1,0:T(8,128)S(1)}, f32[2,2,32,128]{3,2,1,0:T(8,128)S(1)}, u32[]{:S(2)}, u32[]{:S(2)}) collective-permute-start(f32[2,2,32,128]{3,2,1,0:T(8,128)S(1)} %get-tuple-element.41), channel_id=1, source_target_pairs={{0,3},{1,2},{2,1},{3,0},{4,7},{5,6},{6,5},{7,4},{8,11},{9,10},{10,... | collective-permute-start | bytes 196616 | tf_op jit(solution)/shard_map/ppermute | solution.py:379
  12.3 0.7 %copy-start.5 = (s32[1,8,2]{1,2,0:T(2,128)S(1)}, s32[1,8,2]{1,2,0:T(2,128)}, u32[]{:S(2)}) copy-start(s32[1,8,2]{1,2,0:T(2,128)} %param.16) | copy-start | bytes 196
  12.3 0.7 %copy-start.7 = (s32[1,3]{1,0:T(1,128)S(1)}, s32[1,3]{1,0:T(1,128)}, u32[]{:S(2)}) copy-start(s32[1,3]{1,0:T(1,128)} %src.1) | copy-start | bytes 40
  18.7 1.4 %collective-permute-start.8 = (f32[2,136,128]{2,1,0:T(8,128)S(1)}, f32[2,136,128]{2,1,0:T(8,128)S(1)}, u32[]{:S(2)}, u32[]{:S(2)}) collective-permute-start(f32[2,136,128]{2,1,0:T(8,128)S(1)} %get-tuple-element.57), channel_id=1, source_target_pairs={{0,1},{1,0},{2,3},{3,2},{4,5},{5,4},{6,7},{7,6},{8,9},{9,8},{10,11... | collective-permute-start | bytes 417800 | tf_op jit(solution)/shard_map/ppermute | solution.py:379
  20.1 5.3 %collective-permute-start.10 = (f32[136,128]{1,0:T(8,128)S(1)}, f32[136,128]{1,0:T(8,128)S(1)}, u32[]{:S(2)}, u32[]{:S(2)}) collective-permute-start(f32[136,128]{1,0:T(8,128)S(1)} %get-tuple-element.60), channel_id=1, source_target_pairs={{0,6},{1,7},{2,4},{3,5},{4,2},{5,3},{6,0},{7,1},{8,14},{9,15},{10,... | collective-permute-start | bytes 208904 | tf_op jit(solution)/shard_map/ppermute | solution.py:379
  22.5 4.4 %collective-permute-start.11 = (f32[136,128]{1,0:T(8,128)S(1)}, f32[136,128]{1,0:T(8,128)S(1)}, u32[]{:S(2)}, u32[]{:S(2)}) collective-permute-start(f32[136,128]{1,0:T(8,128)S(1)} %get-tuple-element.61), channel_id=1, source_target_pairs={{0,4},{1,5},{2,6},{3,7},{4,0},{5,1},{6,2},{7,3},{8,12},{9,13},{10,... | collective-permute-start | bytes 208904 | tf_op jit(solution)/shard_map/ppermute | solution.py:379
  23.0 4.3 %collective-permute-start.9 = (f32[136,128]{1,0:T(8,128)S(1)}, f32[136,128]{1,0:T(8,128)S(1)}, u32[]{:S(2)}, u32[]{:S(2)}) collective-permute-start(f32[136,128]{1,0:T(8,128)S(1)} %get-tuple-element.59), channel_id=1, source_target_pairs={{0,2},{1,3},{2,0},{3,1},{4,6},{5,7},{6,4},{7,5},{8,10},{9,11},{10,... | collective-permute-start | bytes 208904 | tf_op jit(solution)/shard_map/ppermute | solution.py:379
  27.5 6.4 %collective-permute-start.12 = (f32[2,64,128]{2,1,0:T(8,128)S(1)}, f32[2,64,128]{2,1,0:T(8,128)S(1)}, u32[]{:S(2)}, u32[]{:S(2)}) collective-permute-start(f32[2,64,128]{2,1,0:T(8,128)S(1)} %get-tuple-element.63), channel_id=1, source_target_pairs={{0,24},{8,16},{16,8},{24,0},{1,25},{9,17},{17,9},{25,1},{2,26},{10... | collective-permute-start | bytes 196616 | tf_op jit(solution)/shard_map/ppermute | solution.py:474
  31.2 5.4 %collective-permute-start.13 = (f32[2,64,128]{2,1,0:T(8,128)S(1)}, f32[2,64,128]{2,1,0:T(8,128)S(1)}, u32[]{:S(2)}, u32[]{:S(2)}) collective-permute-start(f32[2,64,128]{2,1,0:T(8,128)S(1)} %get-tuple-element.64), channel_id=1, source_target_pairs={{0,16},{8,24},{16,0},{24,8},{1,17},{9,25},{17,1},{25,9},{2,18},{10... | collective-permute-start | bytes 196616 | tf_op jit(solution)/shard_map/ppermute | solution.py:474
  31.2 5.4 %collective-permute-start.14 = (f32[2,64,128]{2,1,0:T(8,128)S(1)}, f32[2,64,128]{2,1,0:T(8,128)S(1)}, u32[]{:S(2)}, u32[]{:S(2)}) collective-permute-start(f32[2,64,128]{2,1,0:T(8,128)S(1)} %get-tuple-element.65), channel_id=1, source_target_pairs={{0,8},{8,0},{16,24},{24,16},{1,9},{9,1},{17,25},{25,17},{2,10},{10... | collective-permute-start | bytes 196616 | tf_op jit(solution)/shard_map/ppermute | solution.py:474
  36.5 4.0 %collective-permute-start.15 = (f32[64,128]{1,0:T(8,128)S(1)}, f32[64,128]{1,0:T(8,128)S(1)}, u32[]{:S(2)}, u32[]{:S(2)}) collective-permute-start(f32[64,128]{1,0:T(8,128)S(1)} %get-tuple-element.67), channel_id=1, source_target_pairs={{0,4},{1,5},{2,6},{3,7},{4,0},{5,1},{6,2},{7,3},{8,12},{9,13},{10,... | collective-permute-start | bytes 98312 | tf_op jit(solution)/shard_map/ppermute | solution.py:379
  40.5 6.1 %collective-permute-start.16 = (f32[2,64,128]{2,1,0:T(8,128)S(1)}, f32[2,64,128]{2,1,0:T(8,128)S(1)}, u32[]{:S(2)}, u32[]{:S(2)}) collective-permute-start(f32[2,64,128]{2,1,0:T(8,128)S(1)} %gradients.1), channel_id=1, source_target_pairs={{0,24},{8,16},{16,8},{24,0},{1,25},{9,17},{17,9},{25,1},{2,26},{10... | collective-permute-start | bytes 196616 | tf_op jit(solution)/shard_map/ppermute | solution.py:474
  42.9 5.4 %collective-permute-start.17 = (f32[2,64,128]{2,1,0:T(8,128)S(1)}, f32[2,64,128]{2,1,0:T(8,128)S(1)}, u32[]{:S(2)}, u32[]{:S(2)}) collective-permute-start(f32[2,64,128]{2,1,0:T(8,128)S(1)} %gradients.1), channel_id=1, source_target_pairs={{0,16},{8,24},{16,0},{24,8},{1,17},{9,25},{17,1},{25,9},{2,18},{10... | collective-permute-start | bytes 196616 | tf_op jit(solution)/shard_map/ppermute | solution.py:474
  42.9 5.4 %collective-permute-start.18 = (f32[2,64,128]{2,1,0:T(8,128)S(1)}, f32[2,64,128]{2,1,0:T(8,128)S(1)}, u32[]{:S(2)}, u32[]{:S(2)}) collective-permute-start(f32[2,64,128]{2,1,0:T(8,128)S(1)} %gradients.1), channel_id=1, source_target_pairs={{0,8},{8,0},{16,24},{24,16},{1,9},{9,1},{17,25},{25,17},{2,10},{10... | collective-permute-start | bytes 196616 | tf_op jit(solution)/shard_map/ppermute | solution.py:474
